TPU v7x, 256 devices: a whole 4x4x8 slice. The times are simulated.
256 devices in a mesh: dp: 32 (over x, z_hi, core), ctx: 8 (over y, z_lo).
Axes of the slice: x: 4, y: 4, z: 8 (z_hi: 4, z_lo: 2; z = z_hi * 2 + z_lo), core: 2. Of those that a mesh axis runs over, the one named last changes fastest.
Arguments:
- query: bfloat16 [65536, 4096], P(('dp', 'ctx'))
- keys: bfloat16 [65536, 512], P(('dp', 'ctx'))
- values: bfloat16 [65536, 512], P(('dp', 'ctx')), may hold values from -6 to 6
- segments: int32 [65536], P(('dp', 'ctx')), may hold values from 0 to 3, as said below
Outputs:
- attended: bfloat16 [65536, 4096], P(('dp', 'ctx'))
Inputs may be any that keep to these rules, and one draw needn't show every extreme that they name: `segments`: constant over aligned blocks of 128 tokens; within each window of 2048 tokens the numbers start at 0 and rise by one at each document start, so a window holds 1 to 4 documents; some window holds 4.
All inputs are finite; a program needn't handle non-finite values.
Results may differ from a plain program's by a relative error of at most 0.0039.
Values may be sent and summed in bfloat16 or wider, within the bound.
No kernel may reach another device: no remote copies, remote signals or barrier semaphores. Data moves between devices by JAX's collectives and lax.ppermute only.
A program may use at most 64 MiB of HBM per device.

v0:
```python
import functools
import math

import jax
import jax.numpy as jnp
from jax import lax
from jax.experimental import pallas as pl
from jax.experimental.pallas import tpu as pltpu
from jax.sharding import PartitionSpec as P

QH = 32
KVH = 4
HD = 128
TOK = 256
SUB = 128
TAG = 16
PER = QH // KVH
WIDE = KVH * HD
SCALE = math.log2(math.e) / math.sqrt(HD)
SHUT = -1e30
OPEN = 3e38
SAFE = 1e30
START_ROWS = 2 * TOK
VMEM = pl.BlockSpec(memory_space=pltpu.VMEM)
SMEM = pl.BlockSpec(memory_space=pltpu.SMEM)


def aligned(index, size):
    start = index * size
    return pl.ds(start if isinstance(index, int) else pl.multiple_of(start, size), size)


def docs_of(block):
    tag = block[1][TOK : TOK + TAG, :HD].astype(jnp.float32)
    return tag[0:1], tag[8:9]


def cap_of(own, block):
    row = jnp.concatenate(docs_of(block), axis=1)
    caps = []
    for docs in docs_of(own):
        same = row == jnp.concatenate([docs, docs], axis=1)
        caps.append(jnp.where(same, OPEN, SHUT))
    return caps


def own_cap(own):
    rows = lax.broadcasted_iota(jnp.int32, (SUB, TOK), 0)
    cols = lax.broadcasted_iota(jnp.int32, (SUB, TOK), 1)
    return [
        jnp.where(cols <= rows + half * SUB, jnp.broadcast_to(cap, (SUB, TOK)), SHUT)
        for half, cap in enumerate(cap_of(own, own))
    ]


def capped(scores, caps):
    if not caps:
        return scores
    halves = [
        jnp.minimum(scores[half * SUB : (half + 1) * SUB], cap) for half, cap in enumerate(caps)
    ]
    return jnp.concatenate(halves, axis=0)


def scores_of(rows, keys):
    return lax.dot_general(
        rows, keys, (((1,), (1,)), ((), ())), preferred_element_type=jnp.float32
    )


def weighted(weights, values):
    return jnp.dot(
        weights.astype(jnp.bfloat16),
        jnp.concatenate([values, jnp.ones_like(values)], axis=1),
        preferred_element_type=jnp.float32,
    )


def head_sums(own, query, blocks, caps, head):
    cols = aligned(head // PER, HD)
    rows = query[:, aligned(head, HD)]
    near = rows.astype(jnp.float32) * own[0][:, cols].astype(jnp.float32)
    shift = SCALE * jnp.sum(near, axis=1, keepdims=True)
    total = None
    for (keys, values), cap in zip(blocks, caps):
        scores = capped(scores_of(rows, keys[:, cols]) * SCALE - shift, cap())
        added = weighted(jnp.exp2(scores), values[:TOK, cols])
        total = added if total is None else total + added
    return total


def per_head(own, query, blocks, caps, use, unroll=True):
    if unroll:
        for head in range(QH):
            use(head, head_sums(own, query, blocks, caps, head))
        return

    def one_group(group, carry):
        for at in range(PER):
            head = group * PER + at
            use(head, head_sums(own, query, blocks, caps, head))
        return carry

    lax.fori_loop(0, KVH, one_group, 0)


def stored_caps(own, blocks, store):
    readers = []
    for at, block in enumerate(blocks):
        for half, cap in enumerate(cap_of(own, block)):
            store[at, aligned(half, 8)] = jnp.broadcast_to(cap, (8, TOK))
        readers.append(lambda at=at: [store[at, 8 * half : 8 * half + 1] for half in range(2)])
    return readers


def pack_kernel(segments, keys, values, block, tagged):
    rows = lax.broadcasted_iota(jnp.int32, (TAG, WIDE), 0)
    docs = jnp.where(rows < TAG // 2, segments[0], segments[SUB])
    docs = docs.astype(jnp.float32).astype(jnp.bfloat16)
    block[:TOK] = keys[...]
    for target, start in ((block, TOK), (tagged, 0)):
        target[start : start + TOK] = values[...]
        target[start + TOK :] = docs


def own_kernel(query, block, state):
    own = pair_of(block)

    def put(head, sums):
        state[:TOK, aligned(head, 2 * HD)] = sums

    caps = own_cap(own)
    per_head(own, query, [own], [lambda: caps], put)


def pair_of(block):
    return (block.at[:TOK], block.at[TOK:])


def paired(refs, whole):
    refs = iter(refs)
    return [pair_of(next(refs)) if one else (next(refs), next(refs)) for one in whole]


def flat(blocks):
    arrays = [part for block in blocks for part in (block if isinstance(block, tuple) else [block])]
    return arrays, tuple(not isinstance(block, tuple) for block in blocks)


def earlier(steps):
    place = lax.axis_index("ctx")
    y, z = place // 2, place % 2
    return [((y + dy) % 4 * 2 + (z + dz) % 2 < place).astype(jnp.int32) for dy, dz in steps]


def more_kernel(steps, whole, query, *refs):
    count = len(steps)
    own, *blocks = paired(refs[:-3], whole)
    state_in, state, store = refs[-3:]
    flags = earlier(steps)
    every = flags[0]
    for at in range(1, count):
        every = every * flags[at]

    def add(head, sums):
        span = aligned(head, 2 * HD)
        state[:TOK, span] = state_in[:TOK, span] + sums

    def add_again(head, sums):
        state[:TOK, aligned(head, 2 * HD)] += sums

    @pl.when(every > 0)
    def _():
        per_head(own, query, blocks, stored_caps(own, blocks, store), add)

    @pl.when(every == 0)
    def _():
        state[:TOK] = state_in[:TOK]
        for at in range(count):

            @pl.when(flags[at] > 0)
            def _():
                one = [blocks[at]]
                per_head(own, query, one, stored_caps(own, one, store), add_again, unroll=False)


def last_kernel(steps, whole, query, *refs):
    own, *blocks = paired(refs[:-6], whole)
    state, out, merged, worst, store, sem = refs[-6:]
    flags = earlier(steps)
    pieces = [(at * PER * HD, PER * HD) for at in range(KVH - 1)]
    pieces += [((QH - PER + 2 * at) * HD, 2 * HD) for at in range(PER // 2)]

    def out_copy(at):
        span = pl.ds(*pieces[at])
        return pltpu.make_async_copy(merged.at[:, span], out.at[:, span], sem.at[at])

    def put(head, sums):
        merged[:, aligned(head, HD)] = (sums[:, :HD] / sums[:, HD:]).astype(jnp.bfloat16)

    highs = []

    def finish(head, sums):
        sums = sums + state[:TOK, aligned(head, 2 * HD)]
        put(head, sums)
        high = jnp.where(sums[:, HD:] < SAFE, 0.0, 1.0).reshape(TOK // 8, 8, HD)
        highs.append(jnp.max(high, axis=0))
        for at, (start, size) in enumerate(pieces):
            if start + size == (head + 1) * HD:
                out_copy(at).start()
        if head == QH - 1:
            worst[...] = functools.reduce(jnp.maximum, highs)
            highs.clear()

    @pl.when(flags[0] > 0)
    def _():
        per_head(own, query, blocks[:1], stored_caps(own, blocks[:1], store), finish)

    @pl.when(flags[0] == 0)
    def _():
        for head in range(QH):
            finish(head, 0.0)

    bad = jnp.max(worst[...]) > 0.0
    for at in range(len(pieces)):
        out_copy(at).wait()

    @pl.when(bad)
    def _():
        def one_head(head, carry):
            cols = aligned(head // PER, HD)
            rows = query[:, aligned(head, HD)]

            def allowed(block, at):
                scores = scores_of(rows, block[0][:, cols]) * SCALE
                if at is None:
                    return capped(scores, own_cap(own))
                return jnp.where(flags[at] > 0, capped(scores, cap_of(own, block)), SHUT)

            places = [(own, None)] + [(block, at) for at, block in enumerate(blocks)]
            top = None
            for block, at in places:
                high = jnp.max(allowed(block, at), axis=1, keepdims=True)
                top = high if top is None else jnp.maximum(top, high)
            total = jnp.zeros((TOK, 2 * HD), jnp.float32)
            for block, at in places:
                weights = jnp.exp2(allowed(block, at) - top)
                total = total + weighted(weights, block[1][:TOK, cols])
            put(head, total)
            return carry

        lax.fori_loop(0, QH, one_head, 0)
        for at in range(len(pieces)):
            out_copy(at).start()
        for at in range(len(pieces)):
            out_copy(at).wait()


def params():
    return pltpu.CompilerParams(vmem_limit_bytes=8 * 2**20)


def cost(units):
    work = int(units * QH * TOK * TOK)
    return pl.CostEstimate(flops=work * HD * 4, bytes_accessed=2**20, transcendentals=work)


STATE = jax.ShapeDtypeStruct((TOK, 2 * QH * HD), jnp.float32)
START = jax.ShapeDtypeStruct((START_ROWS, 2 * QH * HD), jnp.float32)


def pack(segments, keys, values):
    return pl.pallas_call(
        pack_kernel,
        in_specs=[SMEM, VMEM, VMEM],
        out_specs=(VMEM, VMEM),
        out_shape=(
            jax.ShapeDtypeStruct((2 * TOK + TAG, WIDE), jnp.bfloat16),
            jax.ShapeDtypeStruct((TOK + TAG, WIDE), jnp.bfloat16),
        ),
        name="pack",
    )(segments, keys, values)


def attend_own(query, own):
    return pl.pallas_call(
        own_kernel,
        in_specs=[VMEM] * 2,
        out_specs=VMEM,
        out_shape=START,
        compiler_params=params(),
        cost_estimate=cost(1),
        name="own",
    )(query, own)


def cap_store(count):
    return pltpu.VMEM((count, 16, TOK), jnp.float32)


def attend_more(name, steps, query, own, blocks, state):
    arrays, whole = flat([own] + blocks)
    return pl.pallas_call(
        functools.partial(more_kernel, steps, whole),
        in_specs=[VMEM] * (2 + len(arrays)),
        out_specs=VMEM,
        out_shape=STATE,
        scratch_shapes=[cap_store(len(steps))],
        compiler_params=params(),
        cost_estimate=cost(len(steps)),
        name=name,
    )(query, *arrays, state)


def attend_last(steps, query, own, blocks, state):
    arrays, whole = flat([own] + blocks)
    return pl.pallas_call(
        functools.partial(last_kernel, steps, whole),
        in_specs=[VMEM] * (2 + len(arrays)),
        out_specs=pl.BlockSpec(memory_space=pl.ANY),
        out_shape=jax.ShapeDtypeStruct((TOK, QH * HD), jnp.bfloat16),
        scratch_shapes=[
            pltpu.VMEM((TOK, QH * HD), jnp.bfloat16),
            pltpu.VMEM((8, HD), jnp.float32),
            cap_store(1),
            pltpu.SemaphoreType.DMA((KVH - 1 + PER // 2,)),
        ],
        compiler_params=params(),
        cost_estimate=cost(1),
        name="last",
    )(query, *arrays, state)


def move(value, step_y, step_z):
    pairs = []
    for source in range(8):
        y, z = source // 2, source % 2
        pairs.append((source, (y + step_y) % 4 * 2 + (z + step_z) % 2))
    return lax.ppermute(value, "ctx", pairs)


def local(query, keys, values, segments):
    up = functools.partial(move, step_y=1, step_z=0)
    down = functools.partial(move, step_y=-1, step_z=0)
    over = functools.partial(move, step_y=0, step_z=1)

    k_down, k_over = down(keys), over(keys)
    own, tagged = pack(segments, keys, values)
    v_down, v_over = down(tagged), over(tagged)
    b_up = up(own)
    state = attend_own(query, own)
    v_down, v_over, state = lax.optimization_barrier((v_down, v_over, state))
    b_down = jnp.concatenate([k_down, v_down], axis=0)
    b_over = jnp.concatenate([k_over, v_over], axis=0)
    b_far, b_down_over, b_up_over = down(b_down), over(b_down), up(b_over)
    near = [b_up, (k_down, v_down), (k_over, v_over)]
    near_steps = [(-1, 0), (1, 0), (0, 1)]
    state = attend_more("near", near_steps, query, own, near, state)
    b_far, b_down_over, state = lax.optimization_barrier((b_far, b_down_over, state))
    end = [(over(b_far[:TOK]), down(b_down_over[TOK:]))]
    end_steps = [(2, 1)]
    mid = [b_far, b_up_over, b_down_over]
    mid_steps = [(2, 0), (-1, 1), (1, 1)]
    state = attend_more("mid", mid_steps, query, own, mid, state)
    return attend_last(end_steps + near_steps + mid_steps, query, own, end + near + mid, state)


def solution(mesh):
    placed = (
        P(("dp", "ctx"), None),
        P(("dp", "ctx"), None),
        P(("dp", "ctx"), None),
        P(("dp", "ctx")),
    )
    return jax.shard_map(
        local, mesh=mesh, in_specs=placed, out_specs=P(("dp", "ctx"), None), check_vma=False
    )
```

profile of v0, /device:TPU:22, one launch (start us, length us, event | category | flops | bytes accessed | tf_op | source)
XLA Modules:
  0.0 45.1 jit_solution(13364276973451244196)
XLA Ops:
  0.0 0.4 collective-permute-start
  0.5 2.0 %pack.1 = (bf16[528,512]{1,0:T(8,128)(2,1)}, bf16[272,512]{1,0:T(8,128)(2,1)}) custom-call(s32[256]{0:T(256)} %segments.1, bf16[256,512]{1,0:T(8,128)(2,1)} %keys.1, bf16[256,512]{1,0:T(8,128)(2,1)} %values.1), custom_call_target="tpu_custom_call" | custom-call | tf_op jit(solution)/shard_map/pack/pallas_call | solution.py:273
  2.4 0.4 collective-permute-start.1
  2.9 1.9 %collective-permute-start.2 = (bf16[272,512]{1,0:T(8,128)(2,1)}, bf16[272,512]{1,0:T(8,128)(2,1)S(1)}, u32[]{:S(2)}, u32[]{:S(2)}) collective-permute-start(bf16[272,512]{1,0:T(8,128)(2,1)} %get-tuple-element.14), channel_id=1, source_target_pairs={{0,1},{1,0},{2,3},{3,2},{4,5},{5,4},{6,7},{7,6},{8,9},{9,8},{10,11... | collective-permute-start | bytes 835592 | tf_op jit(solution)/shard_map/ppermute | solution.py:339
  4.8 0.1 collective-permute-start.6
  4.9 1.6 %collective-permute-start.5 = (bf16[528,512]{1,0:T(8,128)(2,1)}, bf16[528,512]{1,0:T(8,128)(2,1)S(1)}, u32[]{:S(2)}, u32[]{:S(2)}) collective-permute-start(bf16[528,512]{1,0:T(8,128)(2,1)} %get-tuple-element.13.block.refs_0_), channel_id=1, source_target_pairs={{0,2},{1,3},{2,4},{3,5},{4,6},{5,7},{6,0},{7,1},{8,10},{9,11},{10,... | collective-permute-start | bytes 1622024 | tf_op jit(solution)/shard_map/ppermute | solution.py:339
  6.5 0.0 copy-start
  6.5 1.6 %copy-done = bf16[256,4096]{1,0:T(8,128)(2,1)S(1)} copy-done((bf16[256,4096]{1,0:T(8,128)(2,1)S(1)}, bf16[256,4096]{1,0:T(8,128)(2,1)}, u32[]{:S(2)}) %copy-start) | copy-done | bytes 2097176
  8.1 0.0 copy-start.2
  8.1 1.0 %copy-done.2 = bf16[528,512]{1,0:T(8,128)(2,1)S(1)} copy-done((bf16[528,512]{1,0:T(8,128)(2,1)S(1)}, bf16[528,512]{1,0:T(8,128)(2,1)}, u32[]{:S(2)}) %copy-start.2) | copy-done | bytes 540696
  9.1 0.0 copy-start.3
  9.1 2.5 %own.1.refs_6_ = f32[512,8192]{1,0:T(8,128)S(1)} custom-call(bf16[256,4096]{1,0:T(8,128)(2,1)S(1)} %copy-done, bf16[528,512]{1,0:T(8,128)(2,1)S(1)} %copy-done.2), custom_call_target="tpu_custom_call" | custom-call | flops 1073741824 | bytes 1048576 | tf_op jit(solution)/shard_map/own/pallas_call | solution.py:286
  11.6 0.0 copy-start.1
  11.6 0.0 collective-permute-done.refs_2_.refs_4_
  11.6 2.6 %collective-permute-done.1.refs_3_.refs_5_ = bf16[272,512]{1,0:T(8,128)(2,1)S(1)} collective-permute-done((bf16[272,512]{1,0:T(8,128)(2,1)}, bf16[272,512]{1,0:T(8,128)(2,1)S(1)}, u32[]{:S(2)}, u32[]{:S(2)}) %collective-permute-start.1) | collective-permute-done | bytes 278560 | tf_op jit(solution)/shard_map/ppermute | solution.py:339
  14.2 0.0 collective-permute-done.2.refs_5_.refs_7_
  14.3 1.5 %collective-permute-start.3 = (bf16[528,512]{1,0:T(8,128)(2,1)S(1)}, bf16[528,512]{1,0:T(8,128)(2,1)S(1)}, u32[]{:S(2)}, u32[]{:S(2)}) collective-permute-start(bf16[528,512]{1,0:T(8,128)(2,1)S(1)} %constant_dynamic-update-slice_fusion), channel_id=1, source_target_pairs={{0,6},{1,7},{2,0},{3,1},{4,2},{5,3},{6,4},{7,5},{8,14},{9,15},{10,... | collective-permute-start | bytes 1622024 | tf_op jit(solution)/shard_map/ppermute | solution.py:339
  15.8 1.9 %collective-permute-start.4 = (bf16[528,512]{1,0:T(8,128)(2,1)S(1)}, bf16[528,512]{1,0:T(8,128)(2,1)S(1)}, u32[]{:S(2)}, u32[]{:S(2)}) collective-permute-start(bf16[528,512]{1,0:T(8,128)(2,1)S(1)} %constant_dynamic-update-slice_fusion), channel_id=1, source_target_pairs={{0,1},{1,0},{2,3},{3,2},{4,5},{5,4},{6,7},{7,6},{8,9},{9,8},{10,11... | collective-permute-start | bytes 1622024 | tf_op jit(solution)/shard_map/ppermute | solution.py:339
  17.7 0.0 collective-permute-done.6.refs_4_.refs_6_
  17.8 1.2 %collective-permute-start.9 = (bf16[528,512]{1,0:T(8,128)(2,1)S(1)}, bf16[528,512]{1,0:T(8,128)(2,1)S(1)}, u32[]{:S(2)}, u32[]{:S(2)}) collective-permute-start(bf16[528,512]{1,0:T(8,128)(2,1)S(1)} %pad_maximum_fusion), channel_id=1, source_target_pairs={{0,2},{1,3},{2,4},{3,5},{4,6},{5,7},{6,0},{7,1},{8,10},{9,11},{10,... | collective-permute-start | bytes 1622024 | tf_op jit(solution)/shard_map/ppermute | solution.py:339
  19.0 0.6 %collective-permute-done.5.refs_1_.refs_3_ = bf16[528,512]{1,0:T(8,128)(2,1)S(1)} collective-permute-done((bf16[528,512]{1,0:T(8,128)(2,1)}, bf16[528,512]{1,0:T(8,128)(2,1)S(1)}, u32[]{:S(2)}, u32[]{:S(2)}) %collective-permute-start.5) | collective-permute-done | bytes 540704 | tf_op jit(solution)/shard_map/ppermute | solution.py:339
  19.6 0.0 copy-done.3
  19.6 0.0 copy-done.1
  19.6 3.9 %near.1.refs_4_ = f32[256,8192]{1,0:T(8,128)S(1)} custom-call(bf16[256,4096]{1,0:T(8,128)(2,1)S(1)} %copy-done.1, bf16[528,512]{1,0:T(8,128)(2,1)S(1)} %copy-done.3, bf16[528,512]{1,0:T(8,128)(2,1)S(1)} %collective-permute-done.5.refs_1_.refs_3_, bf16[256,512]{1,0:T(8,128)(2,1)S(1)} %collective-permute-done.refs_2_.refs_4_, ...), custom_call_target="tpu_custom_call" | custom-call | flops 3221225472 | bytes 1048576 | tf_op jit(solution)/shard_map/near/pallas_call | solution.py:303
  23.5 4.7 %collective-permute-done.3.refs_1_.refs_8_ = bf16[528,512]{1,0:T(8,128)(2,1)S(1)} collective-permute-done((bf16[528,512]{1,0:T(8,128)(2,1)S(1)}, bf16[528,512]{1,0:T(8,128)(2,1)S(1)}, u32[]{:S(2)}, u32[]{:S(2)}) %collective-permute-start.3) | collective-permute-done | bytes 540704 | tf_op jit(solution)/shard_map/ppermute | solution.py:339
  28.2 0.1 collective-permute-done.4.refs_3_.refs_10_
  28.4 3.1 %collective-permute-start.8 = (bf16[272,512]{1,0:T(8,128)(2,1)S(1)}, bf16[272,512]{1,0:T(8,128)(2,1)S(1)}, u32[]{:S(2)}, u32[]{:S(2)}) collective-permute-start(bf16[272,512]{1,0:T(8,128)(2,1)S(1)} %slice.7), channel_id=1, source_target_pairs={{0,6},{1,7},{2,0},{3,1},{4,2},{5,3},{6,4},{7,5},{8,14},{9,15},{10,... | collective-permute-start | bytes 835592 | tf_op jit(solution)/shard_map/ppermute | solution.py:339
  31.5 1.8 %collective-permute-start.7 = (bf16[256,512]{1,0:T(8,128)(2,1)S(1)}, bf16[256,512]{1,0:T(8,128)(2,1)S(1)}, u32[]{:S(2)}, u32[]{:S(2)}) collective-permute-start(bf16[256,512]{1,0:T(8,128)(2,1)S(1)} %slice.6), channel_id=1, source_target_pairs={{0,1},{1,0},{2,3},{3,2},{4,5},{5,4},{6,7},{7,6},{8,9},{9,8},{10,11... | collective-permute-start | bytes 786440 | tf_op jit(solution)/shard_map/ppermute | solution.py:339
  33.3 0.0 collective-permute-done.9.refs_2_.refs_9_
  33.3 7.3 %mid.1.refs_11_ = f32[256,8192]{1,0:T(8,128)S(1)} custom-call(bf16[256,4096]{1,0:T(8,128)(2,1)S(1)} %copy-done.1, bf16[528,512]{1,0:T(8,128)(2,1)S(1)} %copy-done.3, bf16[528,512]{1,0:T(8,128)(2,1)S(1)} %collective-permute-done.3.refs_1_.refs_8_, bf16[528,512]{1,0:T(8,128)(2,1)S(1)} %collective-permute-done.9.refs_2_.refs_9_, ...), custom_call_target="tpu_custom_call" | custom-call | flops 3221225472 | bytes 1048576 | tf_op jit(solution)/shard_map/mid/pallas_call | solution.py:303
  40.5 0.0 collective-permute-done.7.refs_1_
  40.6 0.0 collective-permute-done.8.refs_2_
  40.6 4.3 %last.1 = bf16[256,4096]{1,0:T(8,128)(2,1)} custom-call(bf16[256,4096]{1,0:T(8,128)(2,1)S(1)} %copy-done.1, bf16[528,512]{1,0:T(8,128)(2,1)S(1)} %copy-done.3, bf16[256,512]{1,0:T(8,128)(2,1)S(1)} %collective-permute-done.7.refs_1_, bf16[272,512]{1,0:T(8,128)(2,1)S(1)} %collective-permute-done.8.refs_2_, ...), custom_call_target="tpu_custom_call" | custom-call | flops 1073741824 | bytes 1048576 | tf_op jit(solution)/shard_map/last/pallas_call | solution.py:317
  (5 shorter events, 0.1 us)
Async XLA Ops:
  0.0 11.6 %collective-permute-start = (bf16[256,512]{1,0:T(8,128)(2,1)}, bf16[256,512]{1,0:T(8,128)(2,1)S(1)}, u32[]{:S(2)}, u32[]{:S(2)}) collective-permute-start(bf16[256,512]{1,0:T(8,128)(2,1)} %keys.1), channel_id=1, source_target_pairs={{0,6},{1,7},{2,0},{3,1},{4,2},{5,3},{6,4},{7,5},{8,14},{9,15},{10,... | collective-permute-start | bytes 786440 | tf_op jit(solution)/shard_map/ppermute | solution.py:339
  2.4 11.8 %collective-permute-start.1 = (bf16[272,512]{1,0:T(8,128)(2,1)}, bf16[272,512]{1,0:T(8,128)(2,1)S(1)}, u32[]{:S(2)}, u32[]{:S(2)}) collective-permute-start(bf16[272,512]{1,0:T(8,128)(2,1)} %get-tuple-element.14), channel_id=1, source_target_pairs={{0,6},{1,7},{2,0},{3,1},{4,2},{5,3},{6,4},{7,5},{8,14},{9,15},{10,... | collective-permute-start | bytes 835592 | tf_op jit(solution)/shard_map/ppermute | solution.py:339
  2.9 11.4 %collective-permute-start.2 = (bf16[272,512]{1,0:T(8,128)(2,1)}, bf16[272,512]{1,0:T(8,128)(2,1)S(1)}, u32[]{:S(2)}, u32[]{:S(2)}) collective-permute-start(bf16[272,512]{1,0:T(8,128)(2,1)} %get-tuple-element.14), channel_id=1, source_target_pairs={{0,1},{1,0},{2,3},{3,2},{4,5},{5,4},{6,7},{7,6},{8,9},{9,8},{10,11... | collective-permute-start | bytes 835592 | tf_op jit(solution)/shard_map/ppermute | solution.py:339
  4.8 12.9 %collective-permute-start.6 = (bf16[256,512]{1,0:T(8,128)(2,1)}, bf16[256,512]{1,0:T(8,128)(2,1)S(1)}, u32[]{:S(2)}, u32[]{:S(2)}) collective-permute-start(bf16[256,512]{1,0:T(8,128)(2,1)} %keys.1), channel_id=1, source_target_pairs={{0,1},{1,0},{2,3},{3,2},{4,5},{5,4},{6,7},{7,6},{8,9},{9,8},{10,11... | collective-permute-start | bytes 786440 | tf_op jit(solution)/shard_map/ppermute | solution.py:339
  4.9 14.7 %collective-permute-start.5 = (bf16[528,512]{1,0:T(8,128)(2,1)}, bf16[528,512]{1,0:T(8,128)(2,1)S(1)}, u32[]{:S(2)}, u32[]{:S(2)}) collective-permute-start(bf16[528,512]{1,0:T(8,128)(2,1)} %get-tuple-element.13.block.refs_0_), channel_id=1, source_target_pairs={{0,2},{1,3},{2,4},{3,5},{4,6},{5,7},{6,0},{7,1},{8,10},{9,11},{10,... | collective-permute-start | bytes 1622024 | tf_op jit(solution)/shard_map/ppermute | solution.py:339
  6.5 1.6 %copy-start = (bf16[256,4096]{1,0:T(8,128)(2,1)S(1)}, bf16[256,4096]{1,0:T(8,128)(2,1)}, u32[]{:S(2)}) copy-start(bf16[256,4096]{1,0:T(8,128)(2,1)} %query.7) | copy-start | bytes 6291460
  8.1 1.0 %copy-start.2 = (bf16[528,512]{1,0:T(8,128)(2,1)S(1)}, bf16[528,512]{1,0:T(8,128)(2,1)}, u32[]{:S(2)}) copy-start(bf16[528,512]{1,0:T(8,128)(2,1)} %get-tuple-element.13.block.refs_0_) | copy-start | bytes 1622020
  9.1 10.5 %copy-start.3 = (bf16[528,512]{1,0:T(8,128)(2,1)S(1)}, bf16[528,512]{1,0:T(8,128)(2,1)}, u32[]{:S(2)}) copy-start(bf16[528,512]{1,0:T(8,128)(2,1)} %get-tuple-element.13.block.refs_0_) | copy-start | bytes 1622020
  11.6 8.0 %copy-start.1 = (bf16[256,4096]{1,0:T(8,128)(2,1)S(1)}, bf16[256,4096]{1,0:T(8,128)(2,1)}, u32[]{:S(2)}) copy-start(bf16[256,4096]{1,0:T(8,128)(2,1)} %query.7) | copy-start | bytes 6291460
  14.3 14.0 %collective-permute-start.3 = (bf16[528,512]{1,0:T(8,128)(2,1)S(1)}, bf16[528,512]{1,0:T(8,128)(2,1)S(1)}, u32[]{:S(2)}, u32[]{:S(2)}) collective-permute-start(bf16[528,512]{1,0:T(8,128)(2,1)S(1)} %constant_dynamic-update-slice_fusion), channel_id=1, source_target_pairs={{0,6},{1,7},{2,0},{3,1},{4,2},{5,3},{6,4},{7,5},{8,14},{9,15},{10,... | collective-permute-start | bytes 1622024 | tf_op jit(solution)/shard_map/ppermute | solution.py:339
  15.8 12.5 %collective-permute-start.4 = (bf16[528,512]{1,0:T(8,128)(2,1)S(1)}, bf16[528,512]{1,0:T(8,128)(2,1)S(1)}, u32[]{:S(2)}, u32[]{:S(2)}) collective-permute-start(bf16[528,512]{1,0:T(8,128)(2,1)S(1)} %constant_dynamic-update-slice_fusion), channel_id=1, source_target_pairs={{0,1},{1,0},{2,3},{3,2},{4,5},{5,4},{6,7},{7,6},{8,9},{9,8},{10,11... | collective-permute-start | bytes 1622024 | tf_op jit(solution)/shard_map/ppermute | solution.py:339
  17.8 15.5 %collective-permute-start.9 = (bf16[528,512]{1,0:T(8,128)(2,1)S(1)}, bf16[528,512]{1,0:T(8,128)(2,1)S(1)}, u32[]{:S(2)}, u32[]{:S(2)}) collective-permute-start(bf16[528,512]{1,0:T(8,128)(2,1)S(1)} %pad_maximum_fusion), channel_id=1, source_target_pairs={{0,2},{1,3},{2,4},{3,5},{4,6},{5,7},{6,0},{7,1},{8,10},{9,11},{10,... | collective-permute-start | bytes 1622024 | tf_op jit(solution)/shard_map/ppermute | solution.py:339
  28.4 12.2 %collective-permute-start.8 = (bf16[272,512]{1,0:T(8,128)(2,1)S(1)}, bf16[272,512]{1,0:T(8,128)(2,1)S(1)}, u32[]{:S(2)}, u32[]{:S(2)}) collective-permute-start(bf16[272,512]{1,0:T(8,128)(2,1)S(1)} %slice.7), channel_id=1, source_target_pairs={{0,6},{1,7},{2,0},{3,1},{4,2},{5,3},{6,4},{7,5},{8,14},{9,15},{10,... | collective-permute-start | bytes 835592 | tf_op jit(solution)/shard_map/ppermute | solution.py:339
  31.5 9.1 %collective-permute-start.7 = (bf16[256,512]{1,0:T(8,128)(2,1)S(1)}, bf16[256,512]{1,0:T(8,128)(2,1)S(1)}, u32[]{:S(2)}, u32[]{:S(2)}) collective-permute-start(bf16[256,512]{1,0:T(8,128)(2,1)S(1)} %slice.6), channel_id=1, source_target_pairs={{0,1},{1,0},{2,3},{3,2},{4,5},{5,4},{6,7},{7,6},{8,9},{9,8},{10,11... | collective-permute-start | bytes 786440 | tf_op jit(solution)/shard_map/ppermute | solution.py:339
where the time goes:
time: 45.3 us; the launch traced here: 45.1 us
  Pallas kernels  19.9 us (44%)
  starting transfers between devices  14.1 us (31%)
  waiting for transfers between devices  8.04 us (18%)
  local copies, waits for them, and re-layouts  2.72 us (6%)
    ppermute x10, starting transfers between devices, move(): return lax.ppermute(value, 'ctx', pairs)  14.1 us
    pallas_call x2, Pallas kernels, attend_more(): pl.pallas_call(functools.partial(more_kernel, steps, whole), in_specs=[VM...  11.2 us
    ppermute x10, waiting for transfers between devices, move(): return lax.ppermute(value, 'ctx', pairs)  8.04 us
    pallas_call x1, Pallas kernels, attend_last(): pl.pallas_call(functools.partial(last_kernel, steps, whole), in_specs=[VM...  4.32 us
    unnamed x9, local copies, waits for them, and re-layouts  2.67 us
    pallas_call x1, Pallas kernels, attend_own(): pl.pallas_call(own_kernel, in_specs=[VMEM] * 2, out_specs=VMEM, out_shape...  2.47 us
    pallas_call x1, Pallas kernels, pack(): pl.pallas_call(pack_kernel, in_specs=[SMEM, VMEM, VMEM], out_specs=(VMEM,...  1.97 us
  transfers between devices with their start and end apart: 10, of which 4 were waited for; matrix products, arithmetic and copies ran while one was open for 0% of the time, Pallas kernels for 35%

commit v1 on v0

--- a/solution.py
+++ b/solution.py
@@ -21,6 +21,9 @@
 OPEN = 3e38
 SAFE = 1e30
 START_ROWS = 2 * TOK
+PIECES = ((0, 16), (16, 28), (28, 32))
+NEAR_CASES = (((0, 1, 2), 2), ((0, 1), 1), ((0, 2), 1), ((0,), 1), ((2,), 1))
+MID_CASES = (((0, 1, 2), 4), ((0, 1), 1), ((1,), 1))
 VMEM = pl.BlockSpec(memory_space=pltpu.VMEM)
 SMEM = pl.BlockSpec(memory_space=pltpu.SMEM)
 
@@ -76,8 +79,8 @@
     )
 
 
-def head_sums(own, query, blocks, caps, head):
-    cols = aligned(head // PER, HD)
+def head_sums(own, query, blocks, caps, head, group=None):
+    cols = aligned(head // PER if group is None else group, HD)
     rows = query[:, aligned(head, HD)]
     near = rows.astype(jnp.float32) * own[0][:, cols].astype(jnp.float32)
     shift = SCALE * jnp.sum(near, axis=1, keepdims=True)
@@ -89,19 +92,20 @@
     return total
 
 
-def per_head(own, query, blocks, caps, use, unroll=True):
-    if unroll:
+def per_head(own, query, blocks, caps, use, groups=KVH):
+    if groups == KVH:
         for head in range(QH):
             use(head, head_sums(own, query, blocks, caps, head))
         return
 
-    def one_group(group, carry):
-        for at in range(PER):
-            head = group * PER + at
-            use(head, head_sums(own, query, blocks, caps, head))
+    def some_groups(step, carry):
+        for at in range(groups * PER):
+            head = step * groups * PER + at
+            group = step * groups + at // PER
+            use(head, head_sums(own, query, blocks, caps, head, group))
         return carry
 
-    lax.fori_loop(0, KVH, one_group, 0)
+    lax.fori_loop(0, KVH // groups, some_groups, 0)
 
 
 def stored_caps(own, blocks, store):
@@ -153,43 +157,37 @@
     return [((y + dy) % 4 * 2 + (z + dz) % 2 < place).astype(jnp.int32) for dy, dz in steps]
 
 
-def more_kernel(steps, whole, query, *refs):
+def more_kernel(steps, cases, whole, query, *refs):
     count = len(steps)
     own, *blocks = paired(refs[:-3], whole)
     state_in, state, store = refs[-3:]
     flags = earlier(steps)
-    every = flags[0]
-    for at in range(1, count):
-        every = every * flags[at]
+    code = sum(flag << at for at, flag in enumerate(flags))
 
     def add(head, sums):
         span = aligned(head, 2 * HD)
         state[:TOK, span] = state_in[:TOK, span] + sums
 
-    def add_again(head, sums):
-        state[:TOK, aligned(head, 2 * HD)] += sums
-
-    @pl.when(every > 0)
-    def _():
-        per_head(own, query, blocks, stored_caps(own, blocks, store), add)
-
-    @pl.when(every == 0)
+    rest = jnp.int32(1)
+    for chosen, groups in cases:
+        fits = (code == sum(1 << at for at in chosen)).astype(jnp.int32)
+        rest = rest - fits
+
+        @pl.when(fits > 0)
+        def _():
+            some = [blocks[at] for at in chosen]
+            per_head(own, query, some, stored_caps(own, some, store), add, groups)
+
+    @pl.when(rest > 0)
     def _():
         state[:TOK] = state_in[:TOK]
-        for at in range(count):
-
-            @pl.when(flags[at] > 0)
-            def _():
-                one = [blocks[at]]
-                per_head(own, query, one, stored_caps(own, one, store), add_again, unroll=False)
 
 
 def last_kernel(steps, whole, query, *refs):
     own, *blocks = paired(refs[:-6], whole)
     state, out, merged, worst, store, sem = refs[-6:]
     flags = earlier(steps)
-    pieces = [(at * PER * HD, PER * HD) for at in range(KVH - 1)]
-    pieces += [((QH - PER + 2 * at) * HD, 2 * HD) for at in range(PER // 2)]
+    pieces = [(start * HD, (end - start) * HD) for start, end in PIECES]
 
     def out_copy(at):
         span = pl.ds(*pieces[at])
@@ -298,10 +296,10 @@
     return pltpu.VMEM((count, 16, TOK), jnp.float32)
 
 
-def attend_more(name, steps, query, own, blocks, state):
+def attend_more(name, steps, cases, query, own, blocks, state):
     arrays, whole = flat([own] + blocks)
     return pl.pallas_call(
-        functools.partial(more_kernel, steps, whole),
+        functools.partial(more_kernel, steps, cases, whole),
         in_specs=[VMEM] * (2 + len(arrays)),
         out_specs=VMEM,
         out_shape=STATE,
@@ -323,7 +321,7 @@
             pltpu.VMEM((TOK, QH * HD), jnp.bfloat16),
             pltpu.VMEM((8, HD), jnp.float32),
             cap_store(1),
-            pltpu.SemaphoreType.DMA((KVH - 1 + PER // 2,)),
+            pltpu.SemaphoreType.DMA((len(PIECES),)),
         ],
         compiler_params=params(),
         cost_estimate=cost(1),
@@ -331,11 +329,11 @@
     )(query, *arrays, state)
 
 
-def move(value, step_y, step_z):
+def move(value, step_y, step_z, rows=range(4)):
     pairs = []
-    for source in range(8):
-        y, z = source // 2, source % 2
-        pairs.append((source, (y + step_y) % 4 * 2 + (z + step_z) % 2))
+    for y in rows:
+        for z in range(2):
+            pairs.append((y * 2 + z, (y + step_y) % 4 * 2 + (z + step_z) % 2))
     return lax.ppermute(value, "ctx", pairs)
 
 
@@ -352,16 +350,16 @@
     v_down, v_over, state = lax.optimization_barrier((v_down, v_over, state))
     b_down = jnp.concatenate([k_down, v_down], axis=0)
     b_over = jnp.concatenate([k_over, v_over], axis=0)
-    b_far, b_down_over, b_up_over = down(b_down), over(b_down), up(b_over)
+    b_far, b_down_over, b_up_over = down(b_down), over(b_down), up(b_over, rows=range(3))
     near = [b_up, (k_down, v_down), (k_over, v_over)]
     near_steps = [(-1, 0), (1, 0), (0, 1)]
-    state = attend_more("near", near_steps, query, own, near, state)
+    state = attend_more("near", near_steps, NEAR_CASES, query, own, near, state)
     b_far, b_down_over, state = lax.optimization_barrier((b_far, b_down_over, state))
     end = [(over(b_far[:TOK]), down(b_down_over[TOK:]))]
     end_steps = [(2, 1)]
     mid = [b_far, b_up_over, b_down_over]
     mid_steps = [(2, 0), (-1, 1), (1, 1)]
-    state = attend_more("mid", mid_steps, query, own, mid, state)
+    state = attend_more("mid", mid_steps, MID_CASES, query, own, mid, state)
     return attend_last(end_steps + near_steps + mid_steps, query, own, end + near + mid, state)
 
 

time: 45.3 us -> 44.2 us (0.976)
  starting transfers between devices: 14.1 us -> 15.9 us
  waiting for transfers between devices: 8.04 us -> 6.51 us
  Pallas kernels: 19.9 us -> 18.5 us
    ppermute x10, starting transfers between devices: 14.1 us -> 15.9 us  [move(): return lax.ppermute(value, 'ctx', pairs)]
    ppermute x10, waiting for transfers between devices: 8.04 us -> 6.51 us  [move(): return lax.ppermute(value, 'ctx', pairs)]
    pallas_call x2, Pallas kernels: 11.2 us -> 9.72 us  [attend_more(): pl.pallas_call(functools.partial(more_kernel, steps, cases, whole), in_sp...]
  transfers between devices with their start and end apart: 10 -> 10, of which waited for: 4 -> 3; matrix products, arithmetic and copies ran while one was open for 0% -> 0% of each run, Pallas kernels for 35% -> 32%
where the time goes in v1:
time: 44.2 us; the launch traced here: 44 us
  Pallas kernels  18.5 us (42%)
  starting transfers between devices  15.9 us (36%)
  waiting for transfers between devices  6.51 us (15%)
  local copies, waits for them, and re-layouts  2.72 us (6%)
    ppermute x10, starting transfers between devices, move(): return lax.ppermute(value, 'ctx', pairs)  15.9 us
    pallas_call x2, Pallas kernels, attend_more(): pl.pallas_call(functools.partial(more_kernel, steps, cases, whole), in_sp...  9.72 us
    ppermute x10, waiting for transfers between devices, move(): return lax.ppermute(value, 'ctx', pairs)  6.51 us
    pallas_call x1, Pallas kernels, attend_last(): pl.pallas_call(functools.partial(last_kernel, steps, whole), in_specs=[VM...  4.33 us
    unnamed x9, local copies, waits for them, and re-layouts  2.67 us
    pallas_call x1, Pallas kernels, attend_own(): pl.pallas_call(own_kernel, in_specs=[VMEM] * 2, out_specs=VMEM, out_shape...  2.47 us
    pallas_call x1, Pallas kernels, pack(): pl.pallas_call(pack_kernel, in_specs=[SMEM, VMEM, VMEM], out_specs=(VMEM,...  1.97 us
  transfers between devices with their start and end apart: 10, of which 3 were waited for; matrix products, arithmetic and copies ran while one was open for 0% of the time, Pallas kernels for 32%

profile of v1, /device:TPU:22, one launch (start us, length us, event | category | flops | bytes accessed | tf_op | source)
XLA Modules:
  0.0 44.0 jit_solution(17373171790836443576)
XLA Ops:
  0.0 0.4 %collective-permute-start = (bf16[256,512]{1,0:T(8,128)(2,1)}, bf16[256,512]{1,0:T(8,128)(2,1)S(1)}, u32[]{:S(2)}, u32[]{:S(2)}) collective-permute-start(bf16[256,512]{1,0:T(8,128)(2,1)} %keys.1), channel_id=1, source_target_pairs={{0,6},{1,7},{2,0},{3,1},{4,2},{5,3},{6,4},{7,5},{8,14},{9,15},{10,... | collective-permute-start | bytes 786440 | tf_op jit(solution)/shard_map/ppermute | solution.py:337
  0.5 2.0 %pack.1 = (bf16[528,512]{1,0:T(8,128)(2,1)}, bf16[272,512]{1,0:T(8,128)(2,1)}) custom-call(s32[256]{0:T(256)} %segments.1, bf16[256,512]{1,0:T(8,128)(2,1)} %keys.1, bf16[256,512]{1,0:T(8,128)(2,1)} %values.1), custom_call_target="tpu_custom_call" | custom-call | tf_op jit(solution)/shard_map/pack/pallas_call | solution.py:271
  2.4 0.4 %collective-permute-start.1 = (bf16[272,512]{1,0:T(8,128)(2,1)}, bf16[272,512]{1,0:T(8,128)(2,1)S(1)}, u32[]{:S(2)}, u32[]{:S(2)}) collective-permute-start(bf16[272,512]{1,0:T(8,128)(2,1)} %get-tuple-element.14), channel_id=1, source_target_pairs={{0,6},{1,7},{2,0},{3,1},{4,2},{5,3},{6,4},{7,5},{8,14},{9,15},{10,... | collective-permute-start | bytes 835592 | tf_op jit(solution)/shard_map/ppermute | solution.py:337
  2.9 1.9 %collective-permute-start.2 = (bf16[272,512]{1,0:T(8,128)(2,1)}, bf16[272,512]{1,0:T(8,128)(2,1)S(1)}, u32[]{:S(2)}, u32[]{:S(2)}) collective-permute-start(bf16[272,512]{1,0:T(8,128)(2,1)} %get-tuple-element.14), channel_id=1, source_target_pairs={{0,1},{1,0},{2,3},{3,2},{4,5},{5,4},{6,7},{7,6},{8,9},{9,8},{10,11... | collective-permute-start | bytes 835592 | tf_op jit(solution)/shard_map/ppermute | solution.py:337
  4.8 0.1 collective-permute-start.6
  4.9 1.6 %collective-permute-start.5 = (bf16[528,512]{1,0:T(8,128)(2,1)}, bf16[528,512]{1,0:T(8,128)(2,1)S(1)}, u32[]{:S(2)}, u32[]{:S(2)}) collective-permute-start(bf16[528,512]{1,0:T(8,128)(2,1)} %get-tuple-element.13.block.refs_0_), channel_id=1, source_target_pairs={{0,2},{1,3},{2,4},{3,5},{4,6},{5,7},{6,0},{7,1},{8,10},{9,11},{10,... | collective-permute-start | bytes 1622024 | tf_op jit(solution)/shard_map/ppermute | solution.py:337
  6.5 0.0 copy-start
  6.5 1.6 %copy-done = bf16[256,4096]{1,0:T(8,128)(2,1)S(1)} copy-done((bf16[256,4096]{1,0:T(8,128)(2,1)S(1)}, bf16[256,4096]{1,0:T(8,128)(2,1)}, u32[]{:S(2)}) %copy-start) | copy-done | bytes 2097176
  8.1 0.0 copy-start.2
  8.1 1.0 %copy-done.2 = bf16[528,512]{1,0:T(8,128)(2,1)S(1)} copy-done((bf16[528,512]{1,0:T(8,128)(2,1)S(1)}, bf16[528,512]{1,0:T(8,128)(2,1)}, u32[]{:S(2)}) %copy-start.2) | copy-done | bytes 540696
  9.1 0.0 copy-start.3
  9.1 2.5 %own.1.refs_6_ = f32[512,8192]{1,0:T(8,128)S(1)} custom-call(bf16[256,4096]{1,0:T(8,128)(2,1)S(1)} %copy-done, bf16[528,512]{1,0:T(8,128)(2,1)S(1)} %copy-done.2), custom_call_target="tpu_custom_call" | custom-call | flops 1073741824 | bytes 1048576 | tf_op jit(solution)/shard_map/own/pallas_call | solution.py:284
  11.6 0.0 copy-start.1
  11.6 0.0 collective-permute-done.refs_2_.refs_4_
  11.6 2.6 %collective-permute-done.1.refs_3_.refs_5_ = bf16[272,512]{1,0:T(8,128)(2,1)S(1)} collective-permute-done((bf16[272,512]{1,0:T(8,128)(2,1)}, bf16[272,512]{1,0:T(8,128)(2,1)S(1)}, u32[]{:S(2)}, u32[]{:S(2)}) %collective-permute-start.1) | collective-permute-done | bytes 278560 | tf_op jit(solution)/shard_map/ppermute | solution.py:337
  14.2 0.0 collective-permute-done.2.refs_5_.refs_7_
  14.3 1.5 %collective-permute-start.3 = (bf16[528,512]{1,0:T(8,128)(2,1)S(1)}, bf16[528,512]{1,0:T(8,128)(2,1)S(1)}, u32[]{:S(2)}, u32[]{:S(2)}) collective-permute-start(bf16[528,512]{1,0:T(8,128)(2,1)S(1)} %constant_dynamic-update-slice_fusion), channel_id=1, source_target_pairs={{0,6},{1,7},{2,0},{3,1},{4,2},{5,3},{6,4},{7,5},{8,14},{9,15},{10,... | collective-permute-start | bytes 1622024 | tf_op jit(solution)/shard_map/ppermute | solution.py:337
  15.8 1.9 %collective-permute-start.4 = (bf16[528,512]{1,0:T(8,128)(2,1)S(1)}, bf16[528,512]{1,0:T(8,128)(2,1)S(1)}, u32[]{:S(2)}, u32[]{:S(2)}) collective-permute-start(bf16[528,512]{1,0:T(8,128)(2,1)S(1)} %constant_dynamic-update-slice_fusion), channel_id=1, source_target_pairs={{0,1},{1,0},{2,3},{3,2},{4,5},{5,4},{6,7},{7,6},{8,9},{9,8},{10,11... | collective-permute-start | bytes 1622024 | tf_op jit(solution)/shard_map/ppermute | solution.py:337
  17.7 0.0 collective-permute-done.6.refs_4_.refs_6_
  17.8 3.0 %collective-permute-start.9 = (bf16[528,512]{1,0:T(8,128)(2,1)S(1)}, bf16[528,512]{1,0:T(8,128)(2,1)S(1)}, u32[]{:S(2)}, u32[]{:S(2)}) collective-permute-start(bf16[528,512]{1,0:T(8,128)(2,1)S(1)} %pad_maximum_fusion), channel_id=1, source_target_pairs={{0,2},{1,3},{2,4},{3,5},{4,6},{5,7},{8,10},{9,11},{10,12},{11,13},... | collective-permute-start | bytes 1622024 | tf_op jit(solution)/shard_map/ppermute | solution.py:337
  20.8 0.0 collective-permute-done.5.refs_1_.refs_3_
  20.8 0.0 copy-done.3
  20.8 0.0 copy-done.1
  20.8 3.6 %near.1.refs_4_ = f32[256,8192]{1,0:T(8,128)S(1)} custom-call(bf16[256,4096]{1,0:T(8,128)(2,1)S(1)} %copy-done.1, bf16[528,512]{1,0:T(8,128)(2,1)S(1)} %copy-done.3, bf16[528,512]{1,0:T(8,128)(2,1)S(1)} %collective-permute-done.5.refs_1_.refs_3_, bf16[256,512]{1,0:T(8,128)(2,1)S(1)} %collective-permute-done.refs_2_.refs_4_, ...), custom_call_target="tpu_custom_call" | custom-call | flops 3221225472 | bytes 1048576 | tf_op jit(solution)/shard_map/near/pallas_call | solution.py:301
  24.4 3.8 %collective-permute-done.3.refs_1_.refs_8_ = bf16[528,512]{1,0:T(8,128)(2,1)S(1)} collective-permute-done((bf16[528,512]{1,0:T(8,128)(2,1)S(1)}, bf16[528,512]{1,0:T(8,128)(2,1)S(1)}, u32[]{:S(2)}, u32[]{:S(2)}) %collective-permute-start.3) | collective-permute-done | bytes 540704 | tf_op jit(solution)/shard_map/ppermute | solution.py:337
  28.2 0.1 collective-permute-done.4.refs_3_.refs_10_
  28.4 3.1 %collective-permute-start.8 = (bf16[272,512]{1,0:T(8,128)(2,1)S(1)}, bf16[272,512]{1,0:T(8,128)(2,1)S(1)}, u32[]{:S(2)}, u32[]{:S(2)}) collective-permute-start(bf16[272,512]{1,0:T(8,128)(2,1)S(1)} %slice.7), channel_id=1, source_target_pairs={{0,6},{1,7},{2,0},{3,1},{4,2},{5,3},{6,4},{7,5},{8,14},{9,15},{10,... | collective-permute-start | bytes 835592 | tf_op jit(solution)/shard_map/ppermute | solution.py:337
  31.5 1.8 %collective-permute-start.7 = (bf16[256,512]{1,0:T(8,128)(2,1)S(1)}, bf16[256,512]{1,0:T(8,128)(2,1)S(1)}, u32[]{:S(2)}, u32[]{:S(2)}) collective-permute-start(bf16[256,512]{1,0:T(8,128)(2,1)S(1)} %slice.6), channel_id=1, source_target_pairs={{0,1},{1,0},{2,3},{3,2},{4,5},{5,4},{6,7},{7,6},{8,9},{9,8},{10,11... | collective-permute-start | bytes 786440 | tf_op jit(solution)/shard_map/ppermute | solution.py:337
  33.3 0.0 collective-permute-done.9.refs_2_.refs_9_
  33.3 6.1 %mid.1.refs_11_ = f32[256,8192]{1,0:T(8,128)S(1)} custom-call(bf16[256,4096]{1,0:T(8,128)(2,1)S(1)} %copy-done.1, bf16[528,512]{1,0:T(8,128)(2,1)S(1)} %copy-done.3, bf16[528,512]{1,0:T(8,128)(2,1)S(1)} %collective-permute-done.3.refs_1_.refs_8_, bf16[528,512]{1,0:T(8,128)(2,1)S(1)} %collective-permute-done.9.refs_2_.refs_9_, ...), custom_call_target="tpu_custom_call" | custom-call | flops 3221225472 | bytes 1048576 | tf_op jit(solution)/shard_map/mid/pallas_call | solution.py:301
  39.4 0.0 collective-permute-done.7.refs_1_
  39.4 0.0 collective-permute-done.8.refs_2_
  39.4 4.3 %last.1 = bf16[256,4096]{1,0:T(8,128)(2,1)} custom-call(bf16[256,4096]{1,0:T(8,128)(2,1)S(1)} %copy-done.1, bf16[528,512]{1,0:T(8,128)(2,1)S(1)} %copy-done.3, bf16[256,512]{1,0:T(8,128)(2,1)S(1)} %collective-permute-done.7.refs_1_, bf16[272,512]{1,0:T(8,128)(2,1)S(1)} %collective-permute-done.8.refs_2_, ...), custom_call_target="tpu_custom_call" | custom-call | flops 1073741824 | bytes 1048576 | tf_op jit(solution)/shard_map/last/pallas_call | solution.py:315
  (5 shorter events, 0.1 us)
Async XLA Ops:
  0.0 11.6 %collective-permute-start = (bf16[256,512]{1,0:T(8,128)(2,1)}, bf16[256,512]{1,0:T(8,128)(2,1)S(1)}, u32[]{:S(2)}, u32[]{:S(2)}) collective-permute-start(bf16[256,512]{1,0:T(8,128)(2,1)} %keys.1), channel_id=1, source_target_pairs={{0,6},{1,7},{2,0},{3,1},{4,2},{5,3},{6,4},{7,5},{8,14},{9,15},{10,... | collective-permute-start | bytes 786440 | tf_op jit(solution)/shard_map/ppermute | solution.py:337
  2.4 11.8 %collective-permute-start.1 = (bf16[272,512]{1,0:T(8,128)(2,1)}, bf16[272,512]{1,0:T(8,128)(2,1)S(1)}, u32[]{:S(2)}, u32[]{:S(2)}) collective-permute-start(bf16[272,512]{1,0:T(8,128)(2,1)} %get-tuple-element.14), channel_id=1, source_target_pairs={{0,6},{1,7},{2,0},{3,1},{4,2},{5,3},{6,4},{7,5},{8,14},{9,15},{10,... | collective-permute-start | bytes 835592 | tf_op jit(solution)/shard_map/ppermute | solution.py:337
  2.9 11.4 %collective-permute-start.2 = (bf16[272,512]{1,0:T(8,128)(2,1)}, bf16[272,512]{1,0:T(8,128)(2,1)S(1)}, u32[]{:S(2)}, u32[]{:S(2)}) collective-permute-start(bf16[272,512]{1,0:T(8,128)(2,1)} %get-tuple-element.14), channel_id=1, source_target_pairs={{0,1},{1,0},{2,3},{3,2},{4,5},{5,4},{6,7},{7,6},{8,9},{9,8},{10,11... | collective-permute-start | bytes 835592 | tf_op jit(solution)/shard_map/ppermute | solution.py:337
  4.8 12.9 %collective-permute-start.6 = (bf16[256,512]{1,0:T(8,128)(2,1)}, bf16[256,512]{1,0:T(8,128)(2,1)S(1)}, u32[]{:S(2)}, u32[]{:S(2)}) collective-permute-start(bf16[256,512]{1,0:T(8,128)(2,1)} %keys.1), channel_id=1, source_target_pairs={{0,1},{1,0},{2,3},{3,2},{4,5},{5,4},{6,7},{7,6},{8,9},{9,8},{10,11... | collective-permute-start | bytes 786440 | tf_op jit(solution)/shard_map/ppermute | solution.py:337
  4.9 15.9 %collective-permute-start.5 = (bf16[528,512]{1,0:T(8,128)(2,1)}, bf16[528,512]{1,0:T(8,128)(2,1)S(1)}, u32[]{:S(2)}, u32[]{:S(2)}) collective-permute-start(bf16[528,512]{1,0:T(8,128)(2,1)} %get-tuple-element.13.block.refs_0_), channel_id=1, source_target_pairs={{0,2},{1,3},{2,4},{3,5},{4,6},{5,7},{6,0},{7,1},{8,10},{9,11},{10,... | collective-permute-start | bytes 1622024 | tf_op jit(solution)/shard_map/ppermute | solution.py:337
  6.5 1.6 %copy-start = (bf16[256,4096]{1,0:T(8,128)(2,1)S(1)}, bf16[256,4096]{1,0:T(8,128)(2,1)}, u32[]{:S(2)}) copy-start(bf16[256,4096]{1,0:T(8,128)(2,1)} %query.7) | copy-start | bytes 6291460
  8.1 1.0 %copy-start.2 = (bf16[528,512]{1,0:T(8,128)(2,1)S(1)}, bf16[528,512]{1,0:T(8,128)(2,1)}, u32[]{:S(2)}) copy-start(bf16[528,512]{1,0:T(8,128)(2,1)} %get-tuple-element.13.block.refs_0_) | copy-start | bytes 1622020
  9.1 11.7 %copy-start.3 = (bf16[528,512]{1,0:T(8,128)(2,1)S(1)}, bf16[528,512]{1,0:T(8,128)(2,1)}, u32[]{:S(2)}) copy-start(bf16[528,512]{1,0:T(8,128)(2,1)} %get-tuple-element.13.block.refs_0_) | copy-start | bytes 1622020
  11.6 9.2 %copy-start.1 = (bf16[256,4096]{1,0:T(8,128)(2,1)S(1)}, bf16[256,4096]{1,0:T(8,128)(2,1)}, u32[]{:S(2)}) copy-start(bf16[256,4096]{1,0:T(8,128)(2,1)} %query.7) | copy-start | bytes 6291460
  14.3 14.0 %collective-permute-start.3 = (bf16[528,512]{1,0:T(8,128)(2,1)S(1)}, bf16[528,512]{1,0:T(8,128)(2,1)S(1)}, u32[]{:S(2)}, u32[]{:S(2)}) collective-permute-start(bf16[528,512]{1,0:T(8,128)(2,1)S(1)} %constant_dynamic-update-slice_fusion), channel_id=1, source_target_pairs={{0,6},{1,7},{2,0},{3,1},{4,2},{5,3},{6,4},{7,5},{8,14},{9,15},{10,... | collective-permute-start | bytes 1622024 | tf_op jit(solution)/shard_map/ppermute | solution.py:337
  15.8 12.5 %collective-permute-start.4 = (bf16[528,512]{1,0:T(8,128)(2,1)S(1)}, bf16[528,512]{1,0:T(8,128)(2,1)S(1)}, u32[]{:S(2)}, u32[]{:S(2)}) collective-permute-start(bf16[528,512]{1,0:T(8,128)(2,1)S(1)} %constant_dynamic-update-slice_fusion), channel_id=1, source_target_pairs={{0,1},{1,0},{2,3},{3,2},{4,5},{5,4},{6,7},{7,6},{8,9},{9,8},{10,11... | collective-permute-start | bytes 1622024 | tf_op jit(solution)/shard_map/ppermute | solution.py:337
  17.8 15.5 %collective-permute-start.9 = (bf16[528,512]{1,0:T(8,128)(2,1)S(1)}, bf16[528,512]{1,0:T(8,128)(2,1)S(1)}, u32[]{:S(2)}, u32[]{:S(2)}) collective-permute-start(bf16[528,512]{1,0:T(8,128)(2,1)S(1)} %pad_maximum_fusion), channel_id=1, source_target_pairs={{0,2},{1,3},{2,4},{3,5},{4,6},{5,7},{8,10},{9,11},{10,12},{11,13},... | collective-permute-start | bytes 1622024 | tf_op jit(solution)/shard_map/ppermute | solution.py:337
  28.4 11.1 %collective-permute-start.8 = (bf16[272,512]{1,0:T(8,128)(2,1)S(1)}, bf16[272,512]{1,0:T(8,128)(2,1)S(1)}, u32[]{:S(2)}, u32[]{:S(2)}) collective-permute-start(bf16[272,512]{1,0:T(8,128)(2,1)S(1)} %slice.7), channel_id=1, source_target_pairs={{0,6},{1,7},{2,0},{3,1},{4,2},{5,3},{6,4},{7,5},{8,14},{9,15},{10,... | collective-permute-start | bytes 835592 | tf_op jit(solution)/shard_map/ppermute | solution.py:337
  31.5 7.9 %collective-permute-start.7 = (bf16[256,512]{1,0:T(8,128)(2,1)S(1)}, bf16[256,512]{1,0:T(8,128)(2,1)S(1)}, u32[]{:S(2)}, u32[]{:S(2)}) collective-permute-start(bf16[256,512]{1,0:T(8,128)(2,1)S(1)} %slice.6), channel_id=1, source_target_pairs={{0,1},{1,0},{2,3},{3,2},{4,5},{5,4},{6,7},{7,6},{8,9},{9,8},{10,11... | collective-permute-start | bytes 786440 | tf_op jit(solution)/shard_map/ppermute | solution.py:337

commit v2 on v1

--- a/solution.py
+++ b/solution.py
@@ -23,7 +23,7 @@
 START_ROWS = 2 * TOK
 PIECES = ((0, 16), (16, 28), (28, 32))
 NEAR_CASES = (((0, 1, 2), 2), ((0, 1), 1), ((0, 2), 1), ((0,), 1), ((2,), 1))
-MID_CASES = (((0, 1, 2), 4), ((0, 1), 1), ((1,), 1))
+MID_CASES = (((0, 1, 2), 4), ((0, 1), 2), ((1,), 1))
 VMEM = pl.BlockSpec(memory_space=pltpu.VMEM)
 SMEM = pl.BlockSpec(memory_space=pltpu.SMEM)
 
@@ -196,19 +196,18 @@
     def put(head, sums):
         merged[:, aligned(head, HD)] = (sums[:, :HD] / sums[:, HD:]).astype(jnp.bfloat16)
 
-    highs = []
+    tops = []
 
     def finish(head, sums):
         sums = sums + state[:TOK, aligned(head, 2 * HD)]
         put(head, sums)
-        high = jnp.where(sums[:, HD:] < SAFE, 0.0, 1.0).reshape(TOK // 8, 8, HD)
-        highs.append(jnp.max(high, axis=0))
+        tops.append(jnp.sum(sums[:, HD:].reshape(TOK // 8, 8, HD), axis=0))
         for at, (start, size) in enumerate(pieces):
             if start + size == (head + 1) * HD:
                 out_copy(at).start()
         if head == QH - 1:
-            worst[...] = functools.reduce(jnp.maximum, highs)
-            highs.clear()
+            worst[...] = jnp.where(sum(tops) < SAFE, 0.0, 1.0)
+            tops.clear()
 
     @pl.when(flags[0] > 0)
     def _():

time: 44.2 us -> 43.7 us (0.989); the launches traced: 44 us -> 43 us
  Pallas kernels: 18.5 us -> 17.5 us
    pallas_call x2, Pallas kernels: 9.72 us -> 9.09 us  [attend_more(): pl.pallas_call(functools.partial(more_kernel, steps, cases, whole), in_sp...]
  transfers between devices with their start and end apart: 10 -> 10, of which waited for: 3 -> 3; matrix products, arithmetic and copies ran while one was open for 0% -> 0% of each run, Pallas kernels for 32% -> 31%
where the time goes in v2:
time: 43.7 us; the launch traced here: 43 us
  Pallas kernels  17.5 us (40%)
  starting transfers between devices  15.9 us (36%)
  waiting for transfers between devices  6.51 us (15%)
  local copies, waits for them, and re-layouts  2.72 us (6%)
    ppermute x10, starting transfers between devices, move(): return lax.ppermute(value, 'ctx', pairs)  15.9 us
    pallas_call x2, Pallas kernels, attend_more(): pl.pallas_call(functools.partial(more_kernel, steps, cases, whole), in_sp...  9.09 us
    ppermute x10, waiting for transfers between devices, move(): return lax.ppermute(value, 'ctx', pairs)  6.51 us
    pallas_call x1, Pallas kernels, attend_last(): pl.pallas_call(functools.partial(last_kernel, steps, whole), in_specs=[VM...  3.96 us
    unnamed x9, local copies, waits for them, and re-layouts  2.67 us
    pallas_call x1, Pallas kernels, attend_own(): pl.pallas_call(own_kernel, in_specs=[VMEM] * 2, out_specs=VMEM, out_shape...  2.47 us
    pallas_call x1, Pallas kernels, pack(): pl.pallas_call(pack_kernel, in_specs=[SMEM, VMEM, VMEM], out_specs=(VMEM,...  1.97 us
  transfers between devices with their start and end apart: 10, of which 3 were waited for; matrix products, arithmetic and copies ran while one was open for 0% of the time, Pallas kernels for 31%

profile of v2, /device:TPU:22, one launch (start us, length us, event | category | flops | bytes accessed | tf_op | source)
XLA Modules:
  0.0 43.0 jit_solution(8842368785847964650)
XLA Ops:
  0.0 0.4 %collective-permute-start = (bf16[256,512]{1,0:T(8,128)(2,1)}, bf16[256,512]{1,0:T(8,128)(2,1)S(1)}, u32[]{:S(2)}, u32[]{:S(2)}) collective-permute-start(bf16[256,512]{1,0:T(8,128)(2,1)} %keys.1), channel_id=1, source_target_pairs={{0,6},{1,7},{2,0},{3,1},{4,2},{5,3},{6,4},{7,5},{8,14},{9,15},{10,... | collective-permute-start | bytes 786440 | tf_op jit(solution)/shard_map/ppermute | solution.py:336
  0.5 2.0 %pack.1 = (bf16[528,512]{1,0:T(8,128)(2,1)}, bf16[272,512]{1,0:T(8,128)(2,1)}) custom-call(s32[256]{0:T(256)} %segments.1, bf16[256,512]{1,0:T(8,128)(2,1)} %keys.1, bf16[256,512]{1,0:T(8,128)(2,1)} %values.1), custom_call_target="tpu_custom_call" | custom-call | tf_op jit(solution)/shard_map/pack/pallas_call | solution.py:270
  2.4 0.4 %collective-permute-start.1 = (bf16[272,512]{1,0:T(8,128)(2,1)}, bf16[272,512]{1,0:T(8,128)(2,1)S(1)}, u32[]{:S(2)}, u32[]{:S(2)}) collective-permute-start(bf16[272,512]{1,0:T(8,128)(2,1)} %get-tuple-element.14), channel_id=1, source_target_pairs={{0,6},{1,7},{2,0},{3,1},{4,2},{5,3},{6,4},{7,5},{8,14},{9,15},{10,... | collective-permute-start | bytes 835592 | tf_op jit(solution)/shard_map/ppermute | solution.py:336
  2.9 1.9 %collective-permute-start.2 = (bf16[272,512]{1,0:T(8,128)(2,1)}, bf16[272,512]{1,0:T(8,128)(2,1)S(1)}, u32[]{:S(2)}, u32[]{:S(2)}) collective-permute-start(bf16[272,512]{1,0:T(8,128)(2,1)} %get-tuple-element.14), channel_id=1, source_target_pairs={{0,1},{1,0},{2,3},{3,2},{4,5},{5,4},{6,7},{7,6},{8,9},{9,8},{10,11... | collective-permute-start | bytes 835592 | tf_op jit(solution)/shard_map/ppermute | solution.py:336
  4.8 0.1 collective-permute-start.6
  4.9 1.6 %collective-permute-start.5 = (bf16[528,512]{1,0:T(8,128)(2,1)}, bf16[528,512]{1,0:T(8,128)(2,1)S(1)}, u32[]{:S(2)}, u32[]{:S(2)}) collective-permute-start(bf16[528,512]{1,0:T(8,128)(2,1)} %get-tuple-element.13.block.refs_0_), channel_id=1, source_target_pairs={{0,2},{1,3},{2,4},{3,5},{4,6},{5,7},{6,0},{7,1},{8,10},{9,11},{10,... | collective-permute-start | bytes 1622024 | tf_op jit(solution)/shard_map/ppermute | solution.py:336
  6.5 0.0 copy-start
  6.5 1.6 %copy-done = bf16[256,4096]{1,0:T(8,128)(2,1)S(1)} copy-done((bf16[256,4096]{1,0:T(8,128)(2,1)S(1)}, bf16[256,4096]{1,0:T(8,128)(2,1)}, u32[]{:S(2)}) %copy-start) | copy-done | bytes 2097176
  8.1 0.0 copy-start.2
  8.1 1.0 %copy-done.2 = bf16[528,512]{1,0:T(8,128)(2,1)S(1)} copy-done((bf16[528,512]{1,0:T(8,128)(2,1)S(1)}, bf16[528,512]{1,0:T(8,128)(2,1)}, u32[]{:S(2)}) %copy-start.2) | copy-done | bytes 540696
  9.1 0.0 copy-start.3
  9.1 2.5 %own.1.refs_6_ = f32[512,8192]{1,0:T(8,128)S(1)} custom-call(bf16[256,4096]{1,0:T(8,128)(2,1)S(1)} %copy-done, bf16[528,512]{1,0:T(8,128)(2,1)S(1)} %copy-done.2), custom_call_target="tpu_custom_call" | custom-call | flops 1073741824 | bytes 1048576 | tf_op jit(solution)/shard_map/own/pallas_call | solution.py:283
  11.6 0.0 copy-start.1
  11.6 0.0 collective-permute-done.refs_2_.refs_4_
  11.6 2.6 %collective-permute-done.1.refs_3_.refs_5_ = bf16[272,512]{1,0:T(8,128)(2,1)S(1)} collective-permute-done((bf16[272,512]{1,0:T(8,128)(2,1)}, bf16[272,512]{1,0:T(8,128)(2,1)S(1)}, u32[]{:S(2)}, u32[]{:S(2)}) %collective-permute-start.1) | collective-permute-done | bytes 278560 | tf_op jit(solution)/shard_map/ppermute | solution.py:336
  14.2 0.0 collective-permute-done.2.refs_5_.refs_7_
  14.3 1.5 %collective-permute-start.3 = (bf16[528,512]{1,0:T(8,128)(2,1)S(1)}, bf16[528,512]{1,0:T(8,128)(2,1)S(1)}, u32[]{:S(2)}, u32[]{:S(2)}) collective-permute-start(bf16[528,512]{1,0:T(8,128)(2,1)S(1)} %constant_dynamic-update-slice_fusion), channel_id=1, source_target_pairs={{0,6},{1,7},{2,0},{3,1},{4,2},{5,3},{6,4},{7,5},{8,14},{9,15},{10,... | collective-permute-start | bytes 1622024 | tf_op jit(solution)/shard_map/ppermute | solution.py:336
  15.8 1.9 %collective-permute-start.4 = (bf16[528,512]{1,0:T(8,128)(2,1)S(1)}, bf16[528,512]{1,0:T(8,128)(2,1)S(1)}, u32[]{:S(2)}, u32[]{:S(2)}) collective-permute-start(bf16[528,512]{1,0:T(8,128)(2,1)S(1)} %constant_dynamic-update-slice_fusion), channel_id=1, source_target_pairs={{0,1},{1,0},{2,3},{3,2},{4,5},{5,4},{6,7},{7,6},{8,9},{9,8},{10,11... | collective-permute-start | bytes 1622024 | tf_op jit(solution)/shard_map/ppermute | solution.py:336
  17.7 0.0 collective-permute-done.6.refs_4_.refs_6_
  17.8 3.0 %collective-permute-start.9 = (bf16[528,512]{1,0:T(8,128)(2,1)S(1)}, bf16[528,512]{1,0:T(8,128)(2,1)S(1)}, u32[]{:S(2)}, u32[]{:S(2)}) collective-permute-start(bf16[528,512]{1,0:T(8,128)(2,1)S(1)} %pad_maximum_fusion), channel_id=1, source_target_pairs={{0,2},{1,3},{2,4},{3,5},{4,6},{5,7},{8,10},{9,11},{10,12},{11,13},... | collective-permute-start | bytes 1622024 | tf_op jit(solution)/shard_map/ppermute | solution.py:336
  20.8 0.0 collective-permute-done.5.refs_1_.refs_3_
  20.8 0.0 copy-done.3
  20.8 0.0 copy-done.1
  20.8 3.6 %near.1.refs_4_ = f32[256,8192]{1,0:T(8,128)S(1)} custom-call(bf16[256,4096]{1,0:T(8,128)(2,1)S(1)} %copy-done.1, bf16[528,512]{1,0:T(8,128)(2,1)S(1)} %copy-done.3, bf16[528,512]{1,0:T(8,128)(2,1)S(1)} %collective-permute-done.5.refs_1_.refs_3_, bf16[256,512]{1,0:T(8,128)(2,1)S(1)} %collective-permute-done.refs_2_.refs_4_, ...), custom_call_target="tpu_custom_call" | custom-call | flops 3221225472 | bytes 1048576 | tf_op jit(solution)/shard_map/near/pallas_call | solution.py:300
  24.4 3.8 %collective-permute-done.3.refs_1_.refs_8_ = bf16[528,512]{1,0:T(8,128)(2,1)S(1)} collective-permute-done((bf16[528,512]{1,0:T(8,128)(2,1)S(1)}, bf16[528,512]{1,0:T(8,128)(2,1)S(1)}, u32[]{:S(2)}, u32[]{:S(2)}) %collective-permute-start.3) | collective-permute-done | bytes 540704 | tf_op jit(solution)/shard_map/ppermute | solution.py:336
  28.2 0.1 collective-permute-done.4.refs_3_.refs_10_
  28.4 3.1 %collective-permute-start.8 = (bf16[272,512]{1,0:T(8,128)(2,1)S(1)}, bf16[272,512]{1,0:T(8,128)(2,1)S(1)}, u32[]{:S(2)}, u32[]{:S(2)}) collective-permute-start(bf16[272,512]{1,0:T(8,128)(2,1)S(1)} %slice.7), channel_id=1, source_target_pairs={{0,6},{1,7},{2,0},{3,1},{4,2},{5,3},{6,4},{7,5},{8,14},{9,15},{10,... | collective-permute-start | bytes 835592 | tf_op jit(solution)/shard_map/ppermute | solution.py:336
  31.5 1.8 %collective-permute-start.7 = (bf16[256,512]{1,0:T(8,128)(2,1)S(1)}, bf16[256,512]{1,0:T(8,128)(2,1)S(1)}, u32[]{:S(2)}, u32[]{:S(2)}) collective-permute-start(bf16[256,512]{1,0:T(8,128)(2,1)S(1)} %slice.6), channel_id=1, source_target_pairs={{0,1},{1,0},{2,3},{3,2},{4,5},{5,4},{6,7},{7,6},{8,9},{9,8},{10,11... | collective-permute-start | bytes 786440 | tf_op jit(solution)/shard_map/ppermute | solution.py:336
  33.3 0.0 collective-permute-done.9.refs_2_.refs_9_
  33.3 5.5 %mid.1.refs_11_ = f32[256,8192]{1,0:T(8,128)S(1)} custom-call(bf16[256,4096]{1,0:T(8,128)(2,1)S(1)} %copy-done.1, bf16[528,512]{1,0:T(8,128)(2,1)S(1)} %copy-done.3, bf16[528,512]{1,0:T(8,128)(2,1)S(1)} %collective-permute-done.3.refs_1_.refs_8_, bf16[528,512]{1,0:T(8,128)(2,1)S(1)} %collective-permute-done.9.refs_2_.refs_9_, ...), custom_call_target="tpu_custom_call" | custom-call | flops 3221225472 | bytes 1048576 | tf_op jit(solution)/shard_map/mid/pallas_call | solution.py:300
  38.8 0.0 collective-permute-done.7.refs_1_
  38.8 0.0 collective-permute-done.8.refs_2_
  38.8 4.0 %last.1 = bf16[256,4096]{1,0:T(8,128)(2,1)} custom-call(bf16[256,4096]{1,0:T(8,128)(2,1)S(1)} %copy-done.1, bf16[528,512]{1,0:T(8,128)(2,1)S(1)} %copy-done.3, bf16[256,512]{1,0:T(8,128)(2,1)S(1)} %collective-permute-done.7.refs_1_, bf16[272,512]{1,0:T(8,128)(2,1)S(1)} %collective-permute-done.8.refs_2_, ...), custom_call_target="tpu_custom_call" | custom-call | flops 1073741824 | bytes 1048576 | tf_op jit(solution)/shard_map/last/pallas_call | solution.py:314
  (5 shorter events, 0.1 us)
Async XLA Ops:
  0.0 11.6 %collective-permute-start = (bf16[256,512]{1,0:T(8,128)(2,1)}, bf16[256,512]{1,0:T(8,128)(2,1)S(1)}, u32[]{:S(2)}, u32[]{:S(2)}) collective-permute-start(bf16[256,512]{1,0:T(8,128)(2,1)} %keys.1), channel_id=1, source_target_pairs={{0,6},{1,7},{2,0},{3,1},{4,2},{5,3},{6,4},{7,5},{8,14},{9,15},{10,... | collective-permute-start | bytes 786440 | tf_op jit(solution)/shard_map/ppermute | solution.py:336
  2.4 11.8 %collective-permute-start.1 = (bf16[272,512]{1,0:T(8,128)(2,1)}, bf16[272,512]{1,0:T(8,128)(2,1)S(1)}, u32[]{:S(2)}, u32[]{:S(2)}) collective-permute-start(bf16[272,512]{1,0:T(8,128)(2,1)} %get-tuple-element.14), channel_id=1, source_target_pairs={{0,6},{1,7},{2,0},{3,1},{4,2},{5,3},{6,4},{7,5},{8,14},{9,15},{10,... | collective-permute-start | bytes 835592 | tf_op jit(solution)/shard_map/ppermute | solution.py:336
  2.9 11.4 %collective-permute-start.2 = (bf16[272,512]{1,0:T(8,128)(2,1)}, bf16[272,512]{1,0:T(8,128)(2,1)S(1)}, u32[]{:S(2)}, u32[]{:S(2)}) collective-permute-start(bf16[272,512]{1,0:T(8,128)(2,1)} %get-tuple-element.14), channel_id=1, source_target_pairs={{0,1},{1,0},{2,3},{3,2},{4,5},{5,4},{6,7},{7,6},{8,9},{9,8},{10,11... | collective-permute-start | bytes 835592 | tf_op jit(solution)/shard_map/ppermute | solution.py:336
  4.8 12.9 %collective-permute-start.6 = (bf16[256,512]{1,0:T(8,128)(2,1)}, bf16[256,512]{1,0:T(8,128)(2,1)S(1)}, u32[]{:S(2)}, u32[]{:S(2)}) collective-permute-start(bf16[256,512]{1,0:T(8,128)(2,1)} %keys.1), channel_id=1, source_target_pairs={{0,1},{1,0},{2,3},{3,2},{4,5},{5,4},{6,7},{7,6},{8,9},{9,8},{10,11... | collective-permute-start | bytes 786440 | tf_op jit(solution)/shard_map/ppermute | solution.py:336
  4.9 15.9 %collective-permute-start.5 = (bf16[528,512]{1,0:T(8,128)(2,1)}, bf16[528,512]{1,0:T(8,128)(2,1)S(1)}, u32[]{:S(2)}, u32[]{:S(2)}) collective-permute-start(bf16[528,512]{1,0:T(8,128)(2,1)} %get-tuple-element.13.block.refs_0_), channel_id=1, source_target_pairs={{0,2},{1,3},{2,4},{3,5},{4,6},{5,7},{6,0},{7,1},{8,10},{9,11},{10,... | collective-permute-start | bytes 1622024 | tf_op jit(solution)/shard_map/ppermute | solution.py:336
  6.5 1.6 %copy-start = (bf16[256,4096]{1,0:T(8,128)(2,1)S(1)}, bf16[256,4096]{1,0:T(8,128)(2,1)}, u32[]{:S(2)}) copy-start(bf16[256,4096]{1,0:T(8,128)(2,1)} %query.7) | copy-start | bytes 6291460
  8.1 1.0 %copy-start.2 = (bf16[528,512]{1,0:T(8,128)(2,1)S(1)}, bf16[528,512]{1,0:T(8,128)(2,1)}, u32[]{:S(2)}) copy-start(bf16[528,512]{1,0:T(8,128)(2,1)} %get-tuple-element.13.block.refs_0_) | copy-start | bytes 1622020
  9.1 11.7 %copy-start.3 = (bf16[528,512]{1,0:T(8,128)(2,1)S(1)}, bf16[528,512]{1,0:T(8,128)(2,1)}, u32[]{:S(2)}) copy-start(bf16[528,512]{1,0:T(8,128)(2,1)} %get-tuple-element.13.block.refs_0_) | copy-start | bytes 1622020
  11.6 9.2 %copy-start.1 = (bf16[256,4096]{1,0:T(8,128)(2,1)S(1)}, bf16[256,4096]{1,0:T(8,128)(2,1)}, u32[]{:S(2)}) copy-start(bf16[256,4096]{1,0:T(8,128)(2,1)} %query.7) | copy-start | bytes 6291460
  14.3 14.0 %collective-permute-start.3 = (bf16[528,512]{1,0:T(8,128)(2,1)S(1)}, bf16[528,512]{1,0:T(8,128)(2,1)S(1)}, u32[]{:S(2)}, u32[]{:S(2)}) collective-permute-start(bf16[528,512]{1,0:T(8,128)(2,1)S(1)} %constant_dynamic-update-slice_fusion), channel_id=1, source_target_pairs={{0,6},{1,7},{2,0},{3,1},{4,2},{5,3},{6,4},{7,5},{8,14},{9,15},{10,... | collective-permute-start | bytes 1622024 | tf_op jit(solution)/shard_map/ppermute | solution.py:336
  15.8 12.5 %collective-permute-start.4 = (bf16[528,512]{1,0:T(8,128)(2,1)S(1)}, bf16[528,512]{1,0:T(8,128)(2,1)S(1)}, u32[]{:S(2)}, u32[]{:S(2)}) collective-permute-start(bf16[528,512]{1,0:T(8,128)(2,1)S(1)} %constant_dynamic-update-slice_fusion), channel_id=1, source_target_pairs={{0,1},{1,0},{2,3},{3,2},{4,5},{5,4},{6,7},{7,6},{8,9},{9,8},{10,11... | collective-permute-start | bytes 1622024 | tf_op jit(solution)/shard_map/ppermute | solution.py:336
  17.8 15.5 %collective-permute-start.9 = (bf16[528,512]{1,0:T(8,128)(2,1)S(1)}, bf16[528,512]{1,0:T(8,128)(2,1)S(1)}, u32[]{:S(2)}, u32[]{:S(2)}) collective-permute-start(bf16[528,512]{1,0:T(8,128)(2,1)S(1)} %pad_maximum_fusion), channel_id=1, source_target_pairs={{0,2},{1,3},{2,4},{3,5},{4,6},{5,7},{8,10},{9,11},{10,12},{11,13},... | collective-permute-start | bytes 1622024 | tf_op jit(solution)/shard_map/ppermute | solution.py:336
  28.4 10.4 %collective-permute-start.8 = (bf16[272,512]{1,0:T(8,128)(2,1)S(1)}, bf16[272,512]{1,0:T(8,128)(2,1)S(1)}, u32[]{:S(2)}, u32[]{:S(2)}) collective-permute-start(bf16[272,512]{1,0:T(8,128)(2,1)S(1)} %slice.7), channel_id=1, source_target_pairs={{0,6},{1,7},{2,0},{3,1},{4,2},{5,3},{6,4},{7,5},{8,14},{9,15},{10,... | collective-permute-start | bytes 835592 | tf_op jit(solution)/shard_map/ppermute | solution.py:336
  31.5 7.3 %collective-permute-start.7 = (bf16[256,512]{1,0:T(8,128)(2,1)S(1)}, bf16[256,512]{1,0:T(8,128)(2,1)S(1)}, u32[]{:S(2)}, u32[]{:S(2)}) collective-permute-start(bf16[256,512]{1,0:T(8,128)(2,1)S(1)} %slice.6), channel_id=1, source_target_pairs={{0,1},{1,0},{2,3},{3,2},{4,5},{5,4},{6,7},{7,6},{8,9},{9,8},{10,11... | collective-permute-start | bytes 786440 | tf_op jit(solution)/shard_map/ppermute | solution.py:336
